TPU v7x, 256 devices: a whole 4x4x8 slice. The times are simulated.
256 devices in a mesh: light: 64 (over y, x_lo, z), tex: 4 (over x_hi, core).
Axes of the slice: x: 4 (x_hi: 2, x_lo: 2; x = x_hi * 2 + x_lo), y: 4, z: 8, core: 2. Of those that a mesh axis runs over, the one named last changes fastest.
Arguments:
- light_ids: int32 [128], P('light'), may hold values from 0 to 255
- tile_offsets: int32 [128], P('light'), may hold values from 0 to 4095
- light_table: bfloat16 [256, 512], replicated, may hold values from -6 to 6
- hyper_weight: bfloat16 [512, 1179648], P(None, ('light', 'tex')), may hold values from -0.25 to 0.25
- features: bfloat16 [128, 64, 48, 256], P('light', 'tex'), may hold values from -6 to 6
- upstream_grad: bfloat16 [128, 64, 48, 256], P('light', 'tex'), may hold values from -3 to 3
Outputs:
- relit: bfloat16 [128, 64, 48, 256], P('light', 'tex')
- feature_grad: bfloat16 [128, 64, 48, 256], P('light', 'tex')
- hyper_grad: bfloat16 [512, 1179648], P(None, ('light', 'tex'))
All inputs are finite; a program needn't handle non-finite values.
Results may differ from a plain program's by a relative error of at most 0.02.
Values may be sent and summed in bfloat16 or wider, within the bound.
A program may use at most 128 MiB of HBM per device.

v0:
```python
import math
import jax
import jax.numpy as jnp
from jax import lax
from jax.sharding import PartitionSpec as P


def padded_2(block, sides, width):
    for axis, dim in sides:
        count = lax.axis_size(axis)
        forward = [(i, i + 1) for i in range(count - 1)]
        backward = [(target, source) for source, target in forward]
        low = lax.ppermute(
            lax.slice_in_dim(block, block.shape[dim] - width, None, axis=dim), axis, forward
        )
        high = lax.ppermute(lax.slice_in_dim(block, 0, width, axis=dim), axis, backward)
        block = jnp.concatenate([low, block, high], axis=dim)
    return block


def smooth_act(values):
    return values * jax.nn.sigmoid(values)


def smooth_slope(values):
    sig = jax.nn.sigmoid(values)
    return sig * (1.0 + values * (1.0 - sig))


def light_codes(light_ids, tile_offsets, light_table):
    halfway = light_table.shape[1] // 2
    onehot = (
        light_ids[:, None] == jnp.arange(light_table.shape[0], dtype=jnp.int32)[None, :]
    ).astype(jnp.bfloat16)
    looked = jnp.dot(onehot, light_table, preferred_element_type=jnp.float32)
    rates = jnp.exp(-math.log(1000.0) * jnp.arange(halfway, dtype=jnp.float32) / halfway)
    angles = tile_offsets.astype(jnp.float32)[:, None] * rates[None, :]
    summed = looked + jnp.concatenate([jnp.sin(angles), jnp.cos(angles)], axis=1)
    return (summed * lax.rsqrt(jnp.mean(summed * summed, axis=1, keepdims=True) + 1e-06)).astype(
        jnp.bfloat16
    )


def build_patches(padded, out_rows):
    columns = padded.shape[2]
    wide = jnp.pad(padded, ((0, 0), (0, 0), (1, 1), (0, 0)))
    pieces = [
        wide[:, row_tap : row_tap + out_rows, col_tap : col_tap + columns, :]
        for row_tap in range(3)
        for col_tap in range(3)
    ]
    return jnp.concatenate(pieces, axis=3)


def apply_conv(patches, kernel):
    return jnp.einsum("lrck,lko->lrco", patches, kernel, preferred_element_type=jnp.float32)


def kernel_grad(patches, upstream):
    return jnp.einsum("lrck,lrco->lko", patches, upstream, preferred_element_type=jnp.float32)


def flipped(kernel):
    lights_here, depth, channels = kernel.shape
    shaped = kernel.reshape(lights_here, 3, 3, channels, channels)
    return shaped[:, ::-1, ::-1].swapaxes(3, 4).reshape(lights_here, depth, channels)


def shards(light_ids, tile_offsets, light_table, hyper_weight, features, upstream_grad):
    lights_dev, rows_dev, channels = (features.shape[0], features.shape[1], features.shape[3])
    scale = 1.0 / math.sqrt(9 * channels)
    kernel_len = 9 * channels * channels
    own_codes = light_codes(light_ids, tile_offsets, light_table)
    all_codes = lax.all_gather(own_codes, "light", axis=0, tiled=True)
    columns = (scale * jnp.dot(all_codes, hyper_weight, preferred_element_type=jnp.float32)).astype(
        jnp.bfloat16
    )
    quarters = lax.all_gather(columns, "tex", axis=1, tiled=True)
    weights = lax.all_to_all(quarters, "light", split_axis=0, concat_axis=1, tiled=True)
    first_kernel = weights[:, :kernel_len].reshape(lights_dev, 9 * channels, channels)
    second_kernel = weights[:, kernel_len:].reshape(lights_dev, 9 * channels, channels)
    padded_in = padded_2(features, (("tex", 1),), 1)
    input_patches = build_patches(padded_in, rows_dev)
    first_pre = apply_conv(input_patches, first_kernel)
    hidden = smooth_act(first_pre).astype(jnp.bfloat16)
    padded_hidden = padded_2(hidden, (("tex", 1),), 1)
    hidden_patches = build_patches(padded_hidden, rows_dev)
    second_pre = apply_conv(hidden_patches, second_kernel)
    relit = smooth_act(second_pre).astype(jnp.bfloat16)
    second_grad = (upstream_grad * smooth_slope(second_pre)).astype(jnp.bfloat16)
    padded_grad = padded_2(second_grad, (("tex", 1),), 1)
    hidden_grad = apply_conv(build_patches(padded_grad, rows_dev), flipped(second_kernel))
    first_grad = (hidden_grad * smooth_slope(first_pre)).astype(jnp.bfloat16)
    padded_first = padded_2(first_grad, (("tex", 1),), 1)
    feature_grad = apply_conv(build_patches(padded_first, rows_dev), flipped(first_kernel)).astype(
        jnp.bfloat16
    )
    first_kgrad = kernel_grad(input_patches, first_grad)
    second_kgrad = kernel_grad(hidden_patches, second_grad)
    grads = jnp.concatenate(
        [first_kgrad.reshape(lights_dev, -1), second_kgrad.reshape(lights_dev, -1)], axis=1
    )
    spread = lax.all_to_all(
        grads.astype(jnp.bfloat16), "light", split_axis=1, concat_axis=0, tiled=True
    ).astype(grads.dtype)
    summed = lax.psum_scatter(spread.astype(jnp.bfloat16), "tex", scatter_dimension=1, tiled=True)
    hyper_grad = (
        scale * jnp.einsum("lz,ls->zs", all_codes, summed, preferred_element_type=jnp.float32)
    ).astype(jnp.bfloat16)
    return (relit, feature_grad, hyper_grad)


def solution(mesh):
    in_specs = (
        P("light"),
        P("light"),
        P(),
        P(None, ("light", "tex")),
        P("light", "tex", None, None),
        P("light", "tex", None, None),
    )
    out_specs = (
        P("light", "tex", None, None),
        P("light", "tex", None, None),
        P(None, ("light", "tex")),
    )
    return jax.shard_map(shards, mesh=mesh, in_specs=in_specs, out_specs=out_specs, check_vma=False)
```

profile of v0, /device:TPU:1, one launch (start us, length us, event | category | flops | bytes accessed | tf_op | source)
XLA Modules:
  0.0 607.9 jit_solution(14286666769212236578)
XLA Ops:
  7.2 0.7 convert_element_type.40
  8.1 1.0 multiply_reduce_fusion
  9.2 132.7 %all-gather = bf16[64,2,512]{2,1,0:T(2,128)(2,1)S(1)} all-gather(bf16[1,2,512]{2,1,0:T(2,128)(2,1)S(1)} %fusion.21), channel_id=1, replica_groups=mesh['light'=64,'tex'=4] {'light'}, dimensions={0}, use_global_device_ids=true | all-gather | bytes 133120 | tf_op jit(solution)/shard_map/all_gather | solution.py:74
  141.9 4.1 fusion
  146.1 65.8 %all-gather.3.cloned.1.call-done = bf16[128,18432]{1,0:T(8,128)(2,1)} async-done(((bf16[128,4608]{1,0:T(8,128)(2,1)}), bf16[128,18432]{1,0:T(8,128)(2,1)}) %all-gather.3.cloned.1.call-update) | async-done | bytes 4718608 | tf_op jit(solution)/shard_map/all_gather | solution.py:78
  212.0 7.9 %all_to_all.26 = bf16[64,2,18432]{2,1,0:T(2,128)(2,1)} reshape(bf16[128,18432]{1,0:T(8,128)(2,1)} %all-gather.3.cloned.1.call-done) | data formatting | bytes 9437184 | tf_op jit(solution)/shard_map/all_to_all | solution.py:79
  219.9 10.6 %all-to-all-start = ((bf16[64,2,18432]{2,1,0:T(2,128)(2,1)}), bf16[64,2,18432]{2,1,0:T(2,128)(2,1)}, u32[]{:S(2)}, u32[]{:S(2)}) async-start(bf16[64,2,18432]{2,1,0:T(2,128)(2,1)} %all_to_all.26), calls=%async_computation | async-start | bytes 9437184 | tf_op jit(solution)/shard_map/all_to_all | solution.py:79
  230.5 4.1 collective-permute-start
  234.7 1.9 collective-permute-start.1
  236.6 4.8 collective-permute-done
  241.4 3.0 collective-permute-done.1
  244.5 0.6 fusion.10
  245.0 1.0 slice_dynamic-update-slice_fusion.23
  246.1 1.1 fusion.18
  247.1 1.3 slice_dynamic-update-slice_fusion.22
  248.4 1.0 slice_dynamic-update-slice_fusion.21
  249.4 1.0 constant_dynamic-update-slice_fusion
  250.4 1.4 slice_dynamic-update-slice_fusion.20
  251.8 1.0 slice_dynamic-update-slice_fusion.19
  252.7 1.0 fusion.17
  253.8 1.3 slice_dynamic-update-slice_fusion.18
  255.1 77.5 %all-to-all-done = bf16[64,2,18432]{2,1,0:T(2,128)(2,1)} async-done(((bf16[64,2,18432]{2,1,0:T(2,128)(2,1)}), bf16[64,2,18432]{2,1,0:T(2,128)(2,1)}, u32[]{:S(2)}, u32[]{:S(2)}) %all-to-all-start) | async-done | bytes 4718624 | tf_op jit(solution)/shard_map/all_to_all | solution.py:79
  332.6 5.5 fusion.25
  338.1 8.0 %multiply_convert_fusion.4 = (bf16[2,16,48,256]{3,2,1,0:T(8,128)(2,1)S(1)}, f32[2,16,48,256]{3,2,1,0:T(8,128)}) fusion(bf16[2,16,48,2304]{3,2,1,0:T(8,128)(2,1)} %slice_dynamic-update-slice_fusion.18, bf16[1,2,2304,256]{3,1,2,0:T(2,128)(2,1)S(1)} %bitcast.80), kind=kOutput, calls=%fused_computation.19 | convolution fusion | flops 1813905408 | bytes 11796480 | tf_op jit(solution)/shard_map/lrck,lko->lrco/dot_general | solution.py:56
  346.2 10.2 %collective-permute-start.2 = (bf16[2,1,48,256]{3,2,1,0:T(8,128)(2,1)S(1)}, bf16[2,1,48,256]{3,2,1,0:T(8,128)(2,1)S(1)}, u32[]{:S(2)}, u32[]{:S(2)}) collective-permute-start(bf16[2,1,48,256]{3,2,1,0:T(8,128)(2,1)S(1)} %get-tuple-element.11), channel_id=1, source_target_pairs={{0,1},{1,2},{2,3},{4,5},{5,6},{6,7},{8,9},{9,10},{10,11},{12,13},{... | collective-permute-start | bytes 147464 | tf_op jit(solution)/shard_map/ppermute | solution.py:13
  356.4 2.2 collective-permute-start.3
  358.6 1.7 copy.26
  360.3 2.8 copy.15
  363.2 1.6 rev.6
  364.8 0.6 select_maximum_fusion.4
  365.5 0.4 slice_dynamic-update-slice_fusion.16
  366.0 0.4 slice_dynamic-update-slice_fusion.14
  366.6 0.4 slice_dynamic-update-slice_fusion.12
  366.9 0.6 copy-done.5
  367.7 3.4 multiply_convert_fusion.2
  371.1 5.1 collective-permute-start.4
  376.3 1.9 collective-permute-start.5
  378.2 4.4 fusion.2
  382.6 3.5 concatenate.78
  386.2 3.8 copy.18
  390.0 0.6 select_maximum_fusion.2
  390.7 0.4 slice_dynamic-update-slice_fusion.10
  391.7 0.4 slice_dynamic-update-slice_fusion.6
  392.1 0.6 copy-done.6
  392.7 0.5 copy-done.8
  393.2 2.3 multiply_convert_fusion.1
  395.5 7.3 %fusion.1 = bf16[2,2304,256]{2,1,0:T(8,128)(2,1)} fusion(bf16[2,16,48,2304]{3,2,1,0:T(8,128)(2,1)} %slice_dynamic-update-slice_fusion.18, bf16[2,16,48,256]{3,2,1,0:T(8,128)(2,1)S(1)} %multiply_convert_fusion.1), kind=kOutput, calls=%fused_computation.6 | convolution fusion | flops 1813118976 | bytes 10223616 | tf_op jit(solution)/shard_map/lrck,lrco->lko/dot_general | solution.py:60
  402.8 3.2 concatenate.77
  406.0 3.9 copy.17
  409.8 10.6 %pad_maximum_fusion = bf16[2,64,18432]{2,0,1:T(2,128)(2,1)} fusion(bf16[2,32,18432]{2,0,1:T(2,128)(2,1)} %copy.18, bf16[2,32,18432]{2,0,1:T(2,128)(2,1)} %copy.17), kind=kLoop, calls=%fused_computation.5 | loop fusion | flops 2359296 | bytes 9437184 | tf_op jit(solution)/shard_map/concatenate | solution.py:100
  420.4 111.9 %all_to_all.35 = bf16[2,64,18432]{2,0,1:T(2,128)(2,1)} all-to-all(bf16[2,64,18432]{2,0,1:T(2,128)(2,1)} %pad_maximum_fusion), channel_id=1, replica_groups=mesh['light'=64,'tex'=4] {'light'}, dimensions={1} | all-to-all | bytes 9437184 | tf_op jit(solution)/shard_map/all_to_all | solution.py:103
  532.3 7.5 %all_to_all.32 = bf16[128,18432]{1,0:T(8,128)(2,1)} reshape(bf16[64,2,18432]{2,1,0:T(2,128)(2,1)} %bitcast.77) | data formatting | bytes 9437184 | tf_op jit(solution)/shard_map/all_to_all | solution.py:103
  539.9 5.4 collective-permute-start.6
  545.3 1.9 collective-permute-start.7
  547.2 2.0 copy.25
  549.2 2.7 copy.16
  551.9 2.0 rev.7
  553.9 0.6 select_maximum_fusion
  554.6 0.4 slice_dynamic-update-slice_fusion.4
  555.1 0.4 slice_dynamic-update-slice_fusion.2
  555.6 0.4 slice_dynamic-update-slice_fusion
  556.0 2.9 convolution_convert_fusion
  558.9 37.0 %reduce-scatter.2.cloned.1.call-done = bf16[128,4608]{1,0:T(8,128)(2,1)} async-done(((bf16[128,18432]{1,0:T(8,128)(2,1)}), bf16[128,4608]{1,0:T(8,128)(2,1)}) %reduce-scatter.2.cloned.1.call-update) | async-done | bytes 1179664 | tf_op jit(solution)/shard_map/reduce_scatter | solution.py:106
  596.0 4.9 multiply_convert_fusion
  (53 shorter events, 2.1 us)
Async XLA Ops:
  7.2 1.0 copy-start
  7.2 204.8 %all-gather.3.cloned.1.call-start = ((), (), s32[]{:S(2)}) async-start(), calls=%async_computation.3 | async-start | bytes 5898240 | tf_op jit(solution)/shard_map/all_gather | solution.py:78
  219.9 10.6 %copy-start.2 = (bf16[2,16,48,256]{3,2,1,0:T(8,128)(2,1)S(1)}, bf16[2,16,48,256]{3,2,1,0:T(8,128)(2,1)}, u32[]{:S(2)}) copy-start(bf16[2,16,48,256]{3,2,1,0:T(8,128)(2,1)} %param.10) | copy-start | bytes 2359300
  219.9 112.7 %all-to-all-start = ((bf16[64,2,18432]{2,1,0:T(2,128)(2,1)}), bf16[64,2,18432]{2,1,0:T(2,128)(2,1)}, u32[]{:S(2)}, u32[]{:S(2)}) async-start(bf16[64,2,18432]{2,1,0:T(2,128)(2,1)} %all_to_all.26), calls=%async_computation | async-start | bytes 9437184 | tf_op jit(solution)/shard_map/all_to_all | solution.py:79
  230.5 365.5 %reduce-scatter.2.cloned.1.call-start = ((), (), s32[]{:S(2)}) async-start(), calls=%async_computation.4 | async-start | bytes 5898240 | tf_op jit(solution)/shard_map/reduce_scatter | solution.py:106
  230.5 10.9 %collective-permute-start = (bf16[2,1,48,256]{3,2,1,0:T(8,128)(2,1)S(1)}, bf16[2,1,48,256]{3,2,1,0:T(8,128)(2,1)S(1)}, u32[]{:S(2)}, u32[]{:S(2)}) collective-permute-start(bf16[2,1,48,256]{3,2,1,0:T(8,128)(2,1)S(1)} %get-tuple-element.13), channel_id=1, source_target_pairs={{0,1},{1,2},{2,3},{4,5},{5,6},{6,7},{8,9},{9,10},{10,11},{12,13},{... | collective-permute-start | bytes 147464 | tf_op jit(solution)/shard_map/ppermute | solution.py:13
  234.7 9.8 %collective-permute-start.1 = (bf16[2,1,48,256]{3,2,1,0:T(8,128)(2,1)S(1)}, bf16[2,1,48,256]{3,2,1,0:T(8,128)(2,1)S(1)}, u32[]{:S(2)}, u32[]{:S(2)}) collective-permute-start(bf16[2,1,48,256]{3,2,1,0:T(8,128)(2,1)S(1)} %get-tuple-element.14), channel_id=1, source_target_pairs={{1,0},{2,1},{3,2},{5,4},{6,5},{7,6},{9,8},{10,9},{11,10},{13,12},{... | collective-permute-start | bytes 147464 | tf_op jit(solution)/shard_map/ppermute | solution.py:16
  338.1 8.0 %copy-start.3 = (bf16[2,589824]{1,0:T(2,128)(2,1)}, bf16[2,589824]{1,0:T(2,128)(2,1)S(1)}, u32[]{:S(2)}) copy-start(bf16[2,589824]{1,0:T(2,128)(2,1)S(1)} %get-tuple-element.4) | copy-start | bytes 7077892
  338.1 20.5 %copy-start.4 = (bf16[2,589824]{1,0:T(2,128)(2,1)}, bf16[2,589824]{1,0:T(2,128)(2,1)S(1)}, u32[]{:S(2)}) copy-start(bf16[2,589824]{1,0:T(2,128)(2,1)S(1)} %get-tuple-element.3) | copy-start | bytes 7077892
  346.2 18.6 %collective-permute-start.2 = (bf16[2,1,48,256]{3,2,1,0:T(8,128)(2,1)S(1)}, bf16[2,1,48,256]{3,2,1,0:T(8,128)(2,1)S(1)}, u32[]{:S(2)}, u32[]{:S(2)}) collective-permute-start(bf16[2,1,48,256]{3,2,1,0:T(8,128)(2,1)S(1)} %get-tuple-element.11), channel_id=1, source_target_pairs={{0,1},{1,2},{2,3},{4,5},{5,6},{6,7},{8,9},{9,10},{10,11},{12,13},{... | collective-permute-start | bytes 147464 | tf_op jit(solution)/shard_map/ppermute | solution.py:13
  356.4 8.4 %collective-permute-start.3 = (bf16[2,1,48,256]{3,2,1,0:T(8,128)(2,1)S(1)}, bf16[2,1,48,256]{3,2,1,0:T(8,128)(2,1)S(1)}, u32[]{:S(2)}, u32[]{:S(2)}) collective-permute-start(bf16[2,1,48,256]{3,2,1,0:T(8,128)(2,1)S(1)} %get-tuple-element.12), channel_id=1, source_target_pairs={{1,0},{2,1},{3,2},{5,4},{6,5},{7,6},{9,8},{10,9},{11,10},{13,12},{... | collective-permute-start | bytes 147464 | tf_op jit(solution)/shard_map/ppermute | solution.py:16
  365.9 1.7 copy-start.5
  365.9 1.8 copy-start.7
  371.1 18.8 %collective-permute-start.4 = (bf16[2,1,48,256]{3,2,1,0:T(8,128)(2,1)S(1)}, bf16[2,1,48,256]{3,2,1,0:T(8,128)(2,1)S(1)}, u32[]{:S(2)}, u32[]{:S(2)}) collective-permute-start(bf16[2,1,48,256]{3,2,1,0:T(8,128)(2,1)S(1)} %get-tuple-element.9), channel_id=1, source_target_pairs={{0,1},{1,2},{2,3},{4,5},{5,6},{6,7},{8,9},{9,10},{10,11},{12,13},{... | collective-permute-start | bytes 147464 | tf_op jit(solution)/shard_map/ppermute | solution.py:13
  376.3 13.7 %collective-permute-start.5 = (bf16[2,1,48,256]{3,2,1,0:T(8,128)(2,1)S(1)}, bf16[2,1,48,256]{3,2,1,0:T(8,128)(2,1)S(1)}, u32[]{:S(2)}, u32[]{:S(2)}) collective-permute-start(bf16[2,1,48,256]{3,2,1,0:T(8,128)(2,1)S(1)} %get-tuple-element.10), channel_id=1, source_target_pairs={{1,0},{2,1},{3,2},{5,4},{6,5},{7,6},{9,8},{10,9},{11,10},{13,12},{... | collective-permute-start | bytes 147464 | tf_op jit(solution)/shard_map/ppermute | solution.py:16
  391.1 1.7 copy-start.6
  391.1 2.1 copy-start.8
  539.9 14.0 %collective-permute-start.6 = (bf16[2,1,48,256]{3,2,1,0:T(8,128)(2,1)S(1)}, bf16[2,1,48,256]{3,2,1,0:T(8,128)(2,1)S(1)}, u32[]{:S(2)}, u32[]{:S(2)}) collective-permute-start(bf16[2,1,48,256]{3,2,1,0:T(8,128)(2,1)S(1)} %get-tuple-element.7), channel_id=1, source_target_pairs={{0,1},{1,2},{2,3},{4,5},{5,6},{6,7},{8,9},{9,10},{10,11},{12,13},{... | collective-permute-start | bytes 147464 | tf_op jit(solution)/shard_map/ppermute | solution.py:13
  545.3 8.6 %collective-permute-start.7 = (bf16[2,1,48,256]{3,2,1,0:T(8,128)(2,1)S(1)}, bf16[2,1,48,256]{3,2,1,0:T(8,128)(2,1)S(1)}, u32[]{:S(2)}, u32[]{:S(2)}) collective-permute-start(bf16[2,1,48,256]{3,2,1,0:T(8,128)(2,1)S(1)} %get-tuple-element.8), channel_id=1, source_target_pairs={{1,0},{2,1},{3,2},{5,4},{6,5},{7,6},{9,8},{10,9},{11,10},{13,12},{... | collective-permute-start | bytes 147464 | tf_op jit(solution)/shard_map/ppermute | solution.py:16
  556.0 44.8 %copy-start.1 = (bf16[256,512]{1,0:T(8,128)(2,1)S(1)}, bf16[256,512]{1,0:T(8,128)(2,1)}, u32[]{:S(2)}) copy-start(bf16[256,512]{1,0:T(8,128)(2,1)} %param.8) | copy-start | bytes 786436
Sparse Core Ops, SparseCore 0:
  146.2 65.6 all-gather.2
  540.0 55.9 reduce-scatter.1
where the time goes:
time: 615 us; the launch traced here: 608 us
  blocking collectives  245 us (40%)
  waiting for transfers between devices  188 us (31%)
  local copies, waits for them, and re-layouts  62.3 us (10%)
  starting transfers between devices  43.5 us (7%)
  matrix products  38.3 us (6%)
  other arithmetic  16.2 us (3%)
  between operations  14.7 us (2%)
    all_gather x1, blocking collectives, shards(): all_codes = lax.all_gather(own_codes, 'light', axis=0, tiled=True)  133 us
    all_to_all x1, blocking collectives, shards(): lax.all_to_all(grads.astype(jnp.bfloat16), 'light', split_axis=1, concat_...  112 us
    all_to_all x1, waiting for transfers between devices, shards(): lax.all_to_all(quarters, 'light', split_axis=0, concat_axis=1, tiled=True)  77.5 us
    all_gather x1, waiting for transfers between devices, shards(): quarters = lax.all_gather(columns, 'tex', axis=1, tiled=True)  65.8 us
    reduce_scatter x1, waiting for transfers between devices, shards(): lax.psum_scatter(spread.astype(jnp.bfloat16), 'tex', scatter_dimension=1,...  37 us
    ppermute x4, starting transfers between devices, padded_2(): lax.ppermute(lax.slice_in_dim(block, block.shape[dim] - width, None, axis...  24.9 us
    dot_general x4, matrix products, apply_conv(): jnp.einsum('lrck,lko->lrco', patches, kernel, preferred_element_type=jnp....  16.6 us
    unnamed x45, local copies, waits for them, and re-layouts  15.4 us
  transfers between devices with their start and end apart: 11, of which 5 were waited for; matrix products, arithmetic and copies ran while one was open for 7% of the time, Pallas kernels for 0%

commit v1 on v0

--- a/solution.py
+++ b/solution.py
@@ -75,7 +75,9 @@
     columns = (scale * jnp.dot(all_codes, hyper_weight, preferred_element_type=jnp.float32)).astype(
         jnp.bfloat16
     )
-    quarters = lax.all_gather(columns, "tex", axis=1, tiled=True)
+    quarters = jnp.concatenate(
+        lax.all_to_all(jnp.stack([columns] * lax.axis_size("tex")), "tex", 0, 0), axis=1
+    )
     weights = lax.all_to_all(quarters, "light", split_axis=0, concat_axis=1, tiled=True)
     first_kernel = weights[:, :kernel_len].reshape(lights_dev, 9 * channels, channels)
     second_kernel = weights[:, kernel_len:].reshape(lights_dev, 9 * channels, channels)

time: 615 us -> 638 us (1.037)
  blocking collectives: 245 us -> 331 us
  waiting for transfers between devices: 188 us -> 123 us
  local copies, waits for them, and re-layouts: 62.3 us -> 72.1 us
  starting transfers between devices: 43.5 us -> 36.4 us
    all_to_all x0 -> x1, blocking collectives: none -> 86.7 us  [shards(): lax.all_to_all(jnp.stack([columns] * lax.axis_size('tex')), 'tex', 0, 0)]
    all_gather x1 -> x0, waiting for transfers between devices: 65.8 us -> none  [shards(): quarters = lax.all_gather(columns, 'tex', axis=1, tiled=True)]
  transfers between devices with their start and end apart: 11 -> 10, of which waited for: 5 -> 4; matrix products, arithmetic and copies ran while one was open for 7% -> 6% of each run, Pallas kernels for 0% -> 0%
where the time goes in v1:
time: 638 us; the launch traced here: 631 us
  blocking collectives  331 us (52%)
  waiting for transfers between devices  123 us (19%)
  local copies, waits for them, and re-layouts  72.1 us (11%)
  matrix products  37.2 us (6%)
  starting transfers between devices  36.4 us (6%)
  other arithmetic  16.2 us (3%)
  between operations  14.8 us (2%)
    all_gather x1, blocking collectives, shards(): all_codes = lax.all_gather(own_codes, 'light', axis=0, tiled=True)  133 us
    all_to_all x1, blocking collectives, shards(): lax.all_to_all(grads.astype(jnp.bfloat16), 'light', split_axis=1, concat_...  112 us
    all_to_all x1, blocking collectives, shards(): lax.all_to_all(jnp.stack([columns] * lax.axis_size('tex')), 'tex', 0, 0)  86.7 us
    all_to_all x1, waiting for transfers between devices, shards(): lax.all_to_all(quarters, 'light', split_axis=0, concat_axis=1, tiled=True)  78.8 us
    reduce_scatter x1, waiting for transfers between devices, shards(): lax.psum_scatter(spread.astype(jnp.bfloat16), 'tex', scatter_dimension=1,...  37 us
    ppermute x4, starting transfers between devices, padded_2(): lax.ppermute(lax.slice_in_dim(block, block.shape[dim] - width, None, axis...  22.3 us
    dot_general x4, matrix products, apply_conv(): jnp.einsum('lrck,lko->lrco', patches, kernel, preferred_element_type=jnp....  16.6 us
    unnamed x45, local copies, waits for them, and re-layouts  15.5 us
  transfers between devices with their start and end apart: 10, of which 4 were waited for; matrix products, arithmetic and copies ran while one was open for 6% of the time, Pallas kernels for 0%

profile of v1, /device:TPU:1, one launch (start us, length us, event | category | flops | bytes accessed | tf_op | source)
XLA Modules:
  0.0 631.2 jit_solution(14141263639598180708)
XLA Ops:
  7.2 0.7 convert_element_type.40
  8.1 1.0 multiply_reduce_fusion
  9.2 132.7 %all-gather = bf16[64,2,512]{2,1,0:T(2,128)(2,1)S(1)} all-gather(bf16[1,2,512]{2,1,0:T(2,128)(2,1)S(1)} %fusion.21), channel_id=1, replica_groups=mesh['light'=64,'tex'=4] {'light'}, dimensions={0}, use_global_device_ids=true | all-gather | bytes 133120 | tf_op jit(solution)/shard_map/all_gather | solution.py:74
  142.0 3.1 fusion
  145.5 86.7 %all_to_all.40 = bf16[4,128,4608]{2,1,0:T(8,128)(2,1)S(1)} all-to-all(bf16[4,128,4608]{2,1,0:T(8,128)(2,1)S(1)} %stack.2), channel_id=1, replica_groups=mesh['light'=64,'tex'=4] {'tex'}, dimensions={0} | all-to-all | bytes 9437184 | tf_op jit(solution)/shard_map/all_to_all | solution.py:79
  232.2 5.8 copy.15
  238.0 11.8 %all_to_all.30 = bf16[64,2,18432]{2,1,0:T(2,128)(2,1)} reshape(bf16[128,4,4608]{2,1,0:T(4,128)(2,1)} %copy.15) | data formatting | bytes 9437184 | tf_op jit(solution)/shard_map/all_to_all | solution.py:81
  249.8 5.8 all-to-all-start.1
  255.7 2.9 collective-permute-start
  258.6 2.4 collective-permute-start.1
  261.1 5.6 collective-permute-done
  266.7 1.8 collective-permute-done.1
  268.4 0.6 fusion.10
  269.0 1.0 slice_dynamic-update-slice_fusion.23
  270.0 1.0 fusion.18
  271.0 1.3 slice_dynamic-update-slice_fusion.22
  272.3 1.0 slice_dynamic-update-slice_fusion.21
  273.4 1.1 constant_dynamic-update-slice_fusion
  274.4 1.3 slice_dynamic-update-slice_fusion.20
  275.8 1.0 slice_dynamic-update-slice_fusion.19
  276.7 1.0 fusion.17
  277.7 1.4 slice_dynamic-update-slice_fusion.18
  279.1 78.8 %all-to-all-done.1 = bf16[64,2,18432]{2,1,0:T(2,128)(2,1)} async-done(((bf16[64,2,18432]{2,1,0:T(2,128)(2,1)}), bf16[64,2,18432]{2,1,0:T(2,128)(2,1)}, u32[]{:S(2)}, u32[]{:S(2)}) %all-to-all-start.1) | async-done | bytes 4718624 | tf_op jit(solution)/shard_map/all_to_all | solution.py:81
  357.8 5.5 fusion.25
  363.4 8.0 %multiply_convert_fusion.4 = (bf16[2,16,48,256]{3,2,1,0:T(8,128)(2,1)S(1)}, f32[2,16,48,256]{3,2,1,0:T(8,128)}) fusion(bf16[2,16,48,2304]{3,2,1,0:T(8,128)(2,1)} %slice_dynamic-update-slice_fusion.18, bf16[1,2,2304,256]{3,1,2,0:T(2,128)(2,1)S(1)} %bitcast.82), kind=kOutput, calls=%fused_computation.19 | convolution fusion | flops 1813905408 | bytes 11796480 | tf_op jit(solution)/shard_map/lrck,lko->lrco/dot_general | solution.py:56
  371.4 8.9 %collective-permute-start.2 = (bf16[2,1,48,256]{3,2,1,0:T(8,128)(2,1)S(1)}, bf16[2,1,48,256]{3,2,1,0:T(8,128)(2,1)S(1)}, u32[]{:S(2)}, u32[]{:S(2)}) collective-permute-start(bf16[2,1,48,256]{3,2,1,0:T(8,128)(2,1)S(1)} %get-tuple-element.11), channel_id=1, source_target_pairs={{0,1},{1,2},{2,3},{4,5},{5,6},{6,7},{8,9},{9,10},{10,11},{12,13},{... | collective-permute-start | bytes 147464 | tf_op jit(solution)/shard_map/ppermute | solution.py:13
  380.3 1.9 collective-permute-start.3
  382.2 1.7 copy.27
  383.9 2.8 copy.16
  386.8 1.6 rev.6
  388.4 0.6 select_maximum_fusion.4
  389.1 0.4 slice_dynamic-update-slice_fusion.16
  389.6 0.4 slice_dynamic-update-slice_fusion.14
  390.1 0.4 slice_dynamic-update-slice_fusion.12
  390.5 0.6 copy-done.5
  391.3 3.4 multiply_convert_fusion.2
  394.7 5.2 collective-permute-start.4
  399.9 1.9 collective-permute-start.5
  401.8 4.4 fusion.2
  406.2 3.2 concatenate.78
  409.4 3.8 copy.19
  413.2 0.6 select_maximum_fusion.2
  413.9 0.4 slice_dynamic-update-slice_fusion.10
  415.0 0.4 slice_dynamic-update-slice_fusion.6
  415.4 0.6 copy-done.6
  416.0 0.5 copy-done.8
  416.4 2.3 multiply_convert_fusion.1
  418.7 7.3 %fusion.1 = bf16[2,2304,256]{2,1,0:T(8,128)(2,1)} fusion(bf16[2,16,48,2304]{3,2,1,0:T(8,128)(2,1)} %slice_dynamic-update-slice_fusion.18, bf16[2,16,48,256]{3,2,1,0:T(8,128)(2,1)S(1)} %multiply_convert_fusion.1), kind=kOutput, calls=%fused_computation.6 | convolution fusion | flops 1813118976 | bytes 10223616 | tf_op jit(solution)/shard_map/lrck,lrco->lko/dot_general | solution.py:60
  426.0 3.2 concatenate.77
  429.2 3.9 copy.18
  433.1 10.6 %pad_maximum_fusion = bf16[2,64,18432]{2,0,1:T(2,128)(2,1)} fusion(bf16[2,32,18432]{2,0,1:T(2,128)(2,1)} %copy.19, bf16[2,32,18432]{2,0,1:T(2,128)(2,1)} %copy.18), kind=kLoop, calls=%fused_computation.5 | loop fusion | flops 2359296 | bytes 9437184 | tf_op jit(solution)/shard_map/concatenate | solution.py:102
  443.7 111.8 %all_to_all.41 = bf16[2,64,18432]{2,0,1:T(2,128)(2,1)} all-to-all(bf16[2,64,18432]{2,0,1:T(2,128)(2,1)} %pad_maximum_fusion), channel_id=1, replica_groups=mesh['light'=64,'tex'=4] {'light'}, dimensions={1} | all-to-all | bytes 9437184 | tf_op jit(solution)/shard_map/all_to_all | solution.py:105
  555.6 7.5 %all_to_all.36 = bf16[128,18432]{1,0:T(8,128)(2,1)} reshape(bf16[64,2,18432]{2,1,0:T(2,128)(2,1)} %bitcast.79) | data formatting | bytes 9437184 | tf_op jit(solution)/shard_map/all_to_all | solution.py:105
  563.1 5.4 collective-permute-start.6
  568.5 1.9 collective-permute-start.7
  570.5 2.0 copy.26
  572.5 2.7 copy.17
  575.2 1.9 rev.7
  577.2 0.6 select_maximum_fusion
  577.9 0.4 slice_dynamic-update-slice_fusion.4
  578.9 0.4 slice_dynamic-update-slice_fusion
  579.3 2.9 convolution_convert_fusion
  582.2 37.0 %reduce-scatter.2.cloned.1.call-done = bf16[128,4608]{1,0:T(8,128)(2,1)} async-done(((bf16[128,18432]{1,0:T(8,128)(2,1)}), bf16[128,4608]{1,0:T(8,128)(2,1)}) %reduce-scatter.2.cloned.1.call-update) | async-done | bytes 1179664 | tf_op jit(solution)/shard_map/reduce_scatter | solution.py:108
  619.2 4.9 multiply_convert_fusion
  (53 shorter events, 2.9 us)
Async XLA Ops:
  7.2 1.0 copy-start
  249.8 5.9 copy-start.2
  249.8 108.1 %all-to-all-start.1 = ((bf16[64,2,18432]{2,1,0:T(2,128)(2,1)}), bf16[64,2,18432]{2,1,0:T(2,128)(2,1)}, u32[]{:S(2)}, u32[]{:S(2)}) async-start(bf16[64,2,18432]{2,1,0:T(2,128)(2,1)} %all_to_all.30), calls=%async_computation.1 | async-start | bytes 9437184 | tf_op jit(solution)/shard_map/all_to_all | solution.py:81
  255.6 363.6 %reduce-scatter.2.cloned.1.call-start = ((), (), s32[]{:S(2)}) async-start(), calls=%async_computation.4 | async-start | bytes 5898240 | tf_op jit(solution)/shard_map/reduce_scatter | solution.py:108
  255.7 11.0 %collective-permute-start = (bf16[2,1,48,256]{3,2,1,0:T(8,128)(2,1)S(1)}, bf16[2,1,48,256]{3,2,1,0:T(8,128)(2,1)S(1)}, u32[]{:S(2)}, u32[]{:S(2)}) collective-permute-start(bf16[2,1,48,256]{3,2,1,0:T(8,128)(2,1)S(1)} %get-tuple-element.13), channel_id=1, source_target_pairs={{0,1},{1,2},{2,3},{4,5},{5,6},{6,7},{8,9},{9,10},{10,11},{12,13},{... | collective-permute-start | bytes 147464 | tf_op jit(solution)/shard_map/ppermute | solution.py:13
  258.6 9.8 %collective-permute-start.1 = (bf16[2,1,48,256]{3,2,1,0:T(8,128)(2,1)S(1)}, bf16[2,1,48,256]{3,2,1,0:T(8,128)(2,1)S(1)}, u32[]{:S(2)}, u32[]{:S(2)}) collective-permute-start(bf16[2,1,48,256]{3,2,1,0:T(8,128)(2,1)S(1)} %get-tuple-element.14), channel_id=1, source_target_pairs={{1,0},{2,1},{3,2},{5,4},{6,5},{7,6},{9,8},{10,9},{11,10},{13,12},{... | collective-permute-start | bytes 147464 | tf_op jit(solution)/shard_map/ppermute | solution.py:16
  363.4 8.1 %copy-start.3 = (bf16[2,589824]{1,0:T(2,128)(2,1)}, bf16[2,589824]{1,0:T(2,128)(2,1)S(1)}, u32[]{:S(2)}) copy-start(bf16[2,589824]{1,0:T(2,128)(2,1)S(1)} %get-tuple-element.4) | copy-start | bytes 7077892
  363.4 18.9 %copy-start.4 = (bf16[2,589824]{1,0:T(2,128)(2,1)}, bf16[2,589824]{1,0:T(2,128)(2,1)S(1)}, u32[]{:S(2)}) copy-start(bf16[2,589824]{1,0:T(2,128)(2,1)S(1)} %get-tuple-element.3) | copy-start | bytes 7077892
  371.4 16.9 %collective-permute-start.2 = (bf16[2,1,48,256]{3,2,1,0:T(8,128)(2,1)S(1)}, bf16[2,1,48,256]{3,2,1,0:T(8,128)(2,1)S(1)}, u32[]{:S(2)}, u32[]{:S(2)}) collective-permute-start(bf16[2,1,48,256]{3,2,1,0:T(8,128)(2,1)S(1)} %get-tuple-element.11), channel_id=1, source_target_pairs={{0,1},{1,2},{2,3},{4,5},{5,6},{6,7},{8,9},{9,10},{10,11},{12,13},{... | collective-permute-start | bytes 147464 | tf_op jit(solution)/shard_map/ppermute | solution.py:13
  380.3 8.1 %collective-permute-start.3 = (bf16[2,1,48,256]{3,2,1,0:T(8,128)(2,1)S(1)}, bf16[2,1,48,256]{3,2,1,0:T(8,128)(2,1)S(1)}, u32[]{:S(2)}, u32[]{:S(2)}) collective-permute-start(bf16[2,1,48,256]{3,2,1,0:T(8,128)(2,1)S(1)} %get-tuple-element.12), channel_id=1, source_target_pairs={{1,0},{2,1},{3,2},{5,4},{6,5},{7,6},{9,8},{10,9},{11,10},{13,12},{... | collective-permute-start | bytes 147464 | tf_op jit(solution)/shard_map/ppermute | solution.py:16
  389.5 1.7 copy-start.5
  389.5 1.8 copy-start.7
  394.7 18.5 %collective-permute-start.4 = (bf16[2,1,48,256]{3,2,1,0:T(8,128)(2,1)S(1)}, bf16[2,1,48,256]{3,2,1,0:T(8,128)(2,1)S(1)}, u32[]{:S(2)}, u32[]{:S(2)}) collective-permute-start(bf16[2,1,48,256]{3,2,1,0:T(8,128)(2,1)S(1)} %get-tuple-element.9), channel_id=1, source_target_pairs={{0,1},{1,2},{2,3},{4,5},{5,6},{6,7},{8,9},{9,10},{10,11},{12,13},{... | collective-permute-start | bytes 147464 | tf_op jit(solution)/shard_map/ppermute | solution.py:13
  399.9 13.3 %collective-permute-start.5 = (bf16[2,1,48,256]{3,2,1,0:T(8,128)(2,1)S(1)}, bf16[2,1,48,256]{3,2,1,0:T(8,128)(2,1)S(1)}, u32[]{:S(2)}, u32[]{:S(2)}) collective-permute-start(bf16[2,1,48,256]{3,2,1,0:T(8,128)(2,1)S(1)} %get-tuple-element.10), channel_id=1, source_target_pairs={{1,0},{2,1},{3,2},{5,4},{6,5},{7,6},{9,8},{10,9},{11,10},{13,12},{... | collective-permute-start | bytes 147464 | tf_op jit(solution)/shard_map/ppermute | solution.py:16
  414.3 1.7 copy-start.6
  414.3 2.1 copy-start.8
  563.1 14.0 %collective-permute-start.6 = (bf16[2,1,48,256]{3,2,1,0:T(8,128)(2,1)S(1)}, bf16[2,1,48,256]{3,2,1,0:T(8,128)(2,1)S(1)}, u32[]{:S(2)}, u32[]{:S(2)}) collective-permute-start(bf16[2,1,48,256]{3,2,1,0:T(8,128)(2,1)S(1)} %get-tuple-element.7), channel_id=1, source_target_pairs={{0,1},{1,2},{2,3},{4,5},{5,6},{6,7},{8,9},{9,10},{10,11},{12,13},{... | collective-permute-start | bytes 147464 | tf_op jit(solution)/shard_map/ppermute | solution.py:13
  568.5 8.6 %collective-permute-start.7 = (bf16[2,1,48,256]{3,2,1,0:T(8,128)(2,1)S(1)}, bf16[2,1,48,256]{3,2,1,0:T(8,128)(2,1)S(1)}, u32[]{:S(2)}, u32[]{:S(2)}) collective-permute-start(bf16[2,1,48,256]{3,2,1,0:T(8,128)(2,1)S(1)} %get-tuple-element.8), channel_id=1, source_target_pairs={{1,0},{2,1},{3,2},{5,4},{6,5},{7,6},{9,8},{10,9},{11,10},{13,12},{... | collective-permute-start | bytes 147464 | tf_op jit(solution)/shard_map/ppermute | solution.py:16
  579.3 44.8 %copy-start.1 = (bf16[256,512]{1,0:T(8,128)(2,1)S(1)}, bf16[256,512]{1,0:T(8,128)(2,1)}, u32[]{:S(2)}) copy-start(bf16[256,512]{1,0:T(8,128)(2,1)} %param.8) | copy-start | bytes 786436
Sparse Core Ops, SparseCore 0:
  563.2 55.9 reduce-scatter.1
